TPU v7x, 32 devices: a whole 2x2x4 slice. The times are simulated.
32 devices in a mesh: seq: 4 (over y, x), exp: 8 (over z, core).
Axes of the slice: x: 2, y: 2, z: 4, core: 2. Of those that a mesh axis runs over, the one named last changes fastest.
Arguments:
- tokens: bfloat16 [2048, 2560], P('exp'), may hold values from -6 to 6
- norm_gain: float32 [2560], replicated, may hold values from 0.1 to 1.9
- routes: int32 [2048, 6], P('exp'), may hold values from 0 to 15, all different within a row; in each aligned block of 256 rows (0 to 255, 256 to 511, ...) at most 97 rows name the same one
- route_weights: bfloat16 [2048, 6], P('exp'), may hold values from 0.049804688 to 0.3984375
- w_gate: bfloat16 [16, 2560, 1536], P('exp', None, 'seq'), may hold values from -0.125 to 0.125
- w_up: bfloat16 [16, 2560, 1536], P('exp', None, 'seq'), may hold values from -0.125 to 0.125
- w_down: bfloat16 [16, 1536, 2560], P('exp', 'seq'), may hold values from -0.15625 to 0.15625
- kv_prefill: bfloat16 [4, 256, 32, 1024], P(None, ('seq', 'exp')), may hold values from -6 to 6
- block_map: int32 [256], P(('seq', 'exp')), may hold values from 0 to 255, as said below
- block_empty: int32 [256], P(('seq', 'exp')), may hold values 0 or 1
Outputs:
- moe_out: bfloat16 [2048, 2560], P('exp', 'seq')
- kv_decode: bfloat16 [4, 256, 32, 1024], P(None, ('seq', 'exp'))
Inputs may be any that keep to these rules, and one draw needn't show every extreme that they name: `routes`: in each aligned block of 256 rows no expert is named by more than 97 rows, a bound that some block reaches. block_map is a permutation of the 256 blocks; a block keeps its index of exp, and each device sends exactly 2 blocks to each device of its seq group, itself included.
All inputs are finite; a program needn't handle non-finite values. No bound on the sum of `block_empty` on one device may be relied on, other than what follows from the above.
Results may differ from a plain program's by a relative error of at most 0.013.
Values may be sent and summed in bfloat16 or wider, within the bound.
A program may use at most 128 MiB of HBM per device.

v0:
```python
import jax
import jax.numpy as jnp
from jax import lax
from jax.sharding import PartitionSpec as P


def passed_along(block, axis, distance):
    devices = range(lax.axis_size(axis))
    route = [((i - distance) % len(devices), i) for i in devices]
    return lax.ppermute(block, axis, route)


def rms_normed(tokens, norm_gain):
    values = tokens.astype(jnp.float32)
    scale = lax.rsqrt(jnp.mean(values * values, axis=-1, keepdims=True) + 1e-06)
    return (values * scale * norm_gain).astype(jnp.bfloat16)


def slot_layout(routes, experts, local_experts, owners, capacity):
    flat_routes = routes.reshape(-1)
    onehot = (flat_routes[:, None] == jnp.arange(experts, dtype=jnp.int32)[None, :]).astype(
        jnp.int32
    )
    before = jnp.cumsum(onehot, axis=0) - onehot
    position = jnp.sum(before * onehot, axis=1)
    owner = flat_routes // local_experts
    local_index = flat_routes % local_experts
    return (local_index * owners + owner) * capacity + position


def fill_slots(normed, slot_index, total_slots, topk):
    row_count = normed.shape[0]
    token_of = jnp.arange(slot_index.shape[0], dtype=jnp.int32) // topk
    source = jnp.full((total_slots,), row_count, jnp.int32).at[slot_index].set(token_of)
    padded = jnp.concatenate([normed, jnp.zeros((1, normed.shape[1]), normed.dtype)], axis=0)
    return padded[source]


def expert_block(rows, w_gate, w_up, w_down):
    gate = jnp.einsum("erd,edf->erf", rows, w_gate, preferred_element_type=jnp.float32)
    upward = jnp.einsum("erd,edf->erf", rows, w_up, preferred_element_type=jnp.float32)
    hidden = (jax.nn.silu(gate) * upward).astype(jnp.bfloat16)
    return jnp.einsum("erf,efd->erd", hidden, w_down, preferred_element_type=jnp.float32).astype(
        jnp.bfloat16
    )


def relayout(kv_prefill, block_map, block_empty):
    layers, blocks, block_rows, kv_width = kv_prefill.shape
    seq_count = lax.axis_size("seq")
    exp_count = lax.axis_size("exp")
    per_peer = blocks // seq_count
    keep = (1 - block_empty).astype(jnp.bfloat16)
    kept = kv_prefill * keep[None, :, None, None]
    peer = block_map // blocks // exp_count
    target = block_map % blocks
    order = jnp.argsort(peer * blocks + jnp.arange(blocks, dtype=jnp.int32))
    outgoing = kept[:, order].reshape(layers, seq_count, per_peer, block_rows, kv_width)
    labels = target[order].astype(jnp.bfloat16).reshape(1, seq_count, per_peer)
    my_seq = lax.axis_index("seq")
    arrived = outgoing
    tags = labels
    for step in range(1, seq_count):
        ahead = (my_seq + step) % seq_count
        piece = lax.dynamic_slice_in_dim(outgoing, ahead, 1, 1)
        label = lax.dynamic_slice_in_dim(labels, ahead, 1, 1)
        piece, label = passed_along((piece, label), "seq", step)
        behind = (my_seq - step + seq_count) % seq_count
        arrived = lax.dynamic_update_slice_in_dim(arrived, piece, behind, 1)
        tags = lax.dynamic_update_slice_in_dim(tags, label, behind, 1)
    arrived = arrived.reshape(layers, blocks, block_rows, kv_width)
    slots = tags.reshape(blocks).astype(jnp.int32)
    return arrived[:, jnp.argsort(slots)]


def per_device(
    tokens,
    norm_gain,
    routes,
    route_weights,
    w_gate,
    w_up,
    w_down,
    kv_prefill,
    block_map,
    block_empty,
):
    local_experts = w_gate.shape[0]
    exp_count = lax.axis_size("exp")
    experts = local_experts * exp_count
    tok_count, topk = routes.shape
    capacity = tok_count * topk // experts + 1
    normed = rms_normed(tokens, norm_gain)
    width = normed.shape[1]
    slot_index = slot_layout(routes, experts, local_experts, exp_count, capacity)
    total_slots = local_experts * exp_count * capacity
    outgoing = fill_slots(normed, slot_index, total_slots, topk).reshape(
        local_experts, exp_count * capacity, width
    )
    arrived = lax.all_to_all(outgoing, "exp", split_axis=1, concat_axis=1, tiled=True)
    partial_value = expert_block(arrived, w_gate, w_up, w_down)
    weights = route_weights.astype(jnp.float32)[:, :, None]
    returned = lax.all_to_all(
        partial_value, "exp", split_axis=1, concat_axis=1, tiled=True
    ).reshape(total_slots, width)
    picked = returned[slot_index].astype(jnp.float32).reshape(tok_count, topk, width)
    terms = jnp.sum(picked * weights, axis=1)
    mixed = lax.psum_scatter(terms.astype(jnp.bfloat16), "seq", scatter_dimension=1, tiled=True)
    kv_decode = relayout(kv_prefill, block_map, block_empty)
    return (mixed, kv_decode)


def solution(mesh):
    in_specs = (
        P("exp", None),
        P(),
        P("exp", None),
        P("exp", None),
        P("exp", None, "seq"),
        P("exp", None, "seq"),
        P("exp", "seq", None),
        P(None, ("seq", "exp"), None, None),
        P(("seq", "exp")),
        P(("seq", "exp")),
    )
    out_specs = (P("exp", "seq"), P(None, ("seq", "exp"), None, None))
    return jax.shard_map(
        per_device, mesh=mesh, in_specs=in_specs, out_specs=out_specs, check_vma=False
    )
```

profile of v0, /device:TPU:0, one launch (start us, length us, event | category | flops | bytes accessed | tf_op | source)
XLA Modules:
  0.0 617.2 jit_solution(10809074252446931142)
XLA Ops:
  7.2 0.9 copy.22
  8.1 0.1 eq.40
  8.3 0.1 eq.36
  8.4 0.1 reshape.186
  8.6 1.7 fusion.4
  10.2 4.5 reduce-window.6
  14.8 0.4 slice_reduce_fusion
  15.2 0.2 reduce-window.9
  15.4 0.1 broadcast_add_fusion
  15.6 6.2 %scatter_custom_fusion = s32[1552]{0:T(1024)S(1)} fusion(s32[1536]{0:T(1024)S(1)} %fusion.19, s32[1536]{0:T(1024)S(1)} %add_select_fusion, s32[]{:T(128)} %constant.124.clone.1), kind=kCustom, calls=%fused_computation.50 | custom fusion | bytes 6212 | tf_op jit(solution)/shard_map/scatter | solution.py:34
  21.9 0.4 fusion.6
  22.4 8.2 %gather_fusion = bf16[1552,2560]{1,0:T(8,128)(2,1)} fusion(bf16[257,2560]{1,0:T(8,128)(2,1)S(1)} %concatenate.3, s32[2048]{0:T(1024)S(1)} %pad_clamp_fusion.1), kind=kCustom, calls=%fused_computation | custom fusion | bytes 15898688 | tf_op jit(solution)/shard_map/gather | solution.py:36
  30.5 42.7 %copy.25 = bf16[2,776,2560]{2,0,1:T(2,128)(2,1)S(1)} copy(bf16[2,776,2560]{2,1,0:T(8,128)(2,1)} %bitcast.31) | data formatting | bytes 15892480 | tf_op jit(solution)/shard_map/reshape | solution.py:97
  73.3 181.0 %all_to_all.10 = bf16[2,776,2560]{2,0,1:T(2,128)(2,1)S(1)} all-to-all(bf16[2,776,2560]{2,0,1:T(2,128)(2,1)S(1)} %copy.25), channel_id=1, replica_groups=mesh['seq'=4,'exp'=8] {'exp'}, dimensions={1} | all-to-all | bytes 15892480 | tf_op jit(solution)/shard_map/all_to_all | solution.py:100
  254.3 3.2 copy-done
  257.5 5.7 fusion.2
  263.2 16.0 %convolution_convert_fusion = bf16[2,776,2560]{2,1,0:T(8,128)(2,1)} fusion(bf16[2,384,2560]{2,1,0:T(8,128)(2,1)} %param.16, f32[2,776,384]{2,1,0:T(8,128)} %fusion.2, bf16[2,2560,384]{2,1,0:T(8,128)(2,1)} %param.15, bf16[2,776,2560]{2,0,1:T(2,128)(2,1)} %copy-done), kind=kOutput, calls=%fused_computation.11 | convolution fusion | flops 6110261248 | bytes 26140672 | tf_op jit(solution)/shard_map/erf,efd->erd/dot_general | solution.py:43
  279.2 43.6 %copy.28 = bf16[2,776,2560]{2,0,1:T(2,128)(2,1)} copy(bf16[2,776,2560]{2,1,0:T(8,128)(2,1)} %convolution_convert_fusion) | data formatting | bytes 15892480 | tf_op jit(solution)/shard_map/convert_element_type | solution.py:43
  322.8 5.0 all-to-all-start.1
  327.9 0.3 reduce-scatter.4.cloned.1.call-start
  328.1 0.1 copy.30
  328.3 174.0 %all-to-all-done.1 = bf16[2,776,2560]{2,0,1:T(2,128)(2,1)} async-done(((bf16[2,776,2560]{2,0,1:T(2,128)(2,1)}), bf16[2,776,2560]{2,0,1:T(2,128)(2,1)}, u32[]{:S(2)}, u32[]{:S(2)}) %all-to-all-start.1) | async-done | bytes 7946272 | tf_op jit(solution)/shard_map/all_to_all | solution.py:103
  502.3 7.7 %copy.29 = bf16[2,776,2560]{2,1,0:T(8,128)(2,1)} copy(bf16[2,776,2560]{2,0,1:T(2,128)(2,1)} %all-to-all-done.1) | data formatting | bytes 15892480 | tf_op jit(solution)/shard_map/all_to_all | solution.py:103
  509.9 19.4 %gather_fusion.1 = bf16[1536,2560]{1,0:T(8,128)(2,1)} fusion(bf16[1552,2560]{1,0:T(8,128)(2,1)} %bitcast.30, s32[2048]{0:T(1024)S(1)} %pad_clamp_fusion), kind=kCustom, calls=%fused_computation.1 | custom fusion | bytes 15734784 | tf_op jit(solution)/shard_map/gather | solution.py:106
  529.3 14.2 %reshape.192 = f32[256,6,2560]{2,1,0:T(8,128)} reshape(bf16[1536,2560]{1,0:T(8,128)(2,1)} %gather_fusion.1) | data formatting | bytes 23592960 | tf_op jit(solution)/shard_map/convert_element_type | solution.py:106
  543.5 11.4 %multiply_reduce_fusion = bf16[256,2560]{1,0:T(8,128)(2,1)S(1)} fusion(f32[256,6,2560]{2,1,0:T(8,128)} %reshape.192, f32[256,6]{1,0:T(8,128)S(1)} %copy.30), kind=kLoop, calls=%fused_computation.6 | loop fusion | flops 7208960 | bytes 17045504 | tf_op jit(solution)/shard_map/reduce_sum | solution.py:107
  555.0 1.5 copy.36
  556.5 1.0 sort.31
  557.5 1.5 broadcast_multiply_fusion
  559.1 2.3 gather_fusion.2
  561.4 1.0 constant_dynamic-slice_fusion.3
  562.4 1.5 collective-permute-start
  563.9 1.5 collective-permute-start.1
  565.4 1.4 collective-permute-start.2
  566.8 0.6 gather_fusion.3
  567.6 0.6 collective-permute-start.3
  568.2 0.5 collective-permute-start.4
  568.7 1.5 copy.32
  570.2 24.2 %collective-permute-done.3 = bf16[1,1,2]{2,1,0:T(2,128)(2,1)S(1)} collective-permute-done((bf16[1,1,2]{2,1,0:T(2,128)(2,1)S(1)}, bf16[1,1,2]{2,1,0:T(2,128)(2,1)S(1)}, u32[]{:S(2)}, u32[]{:S(2)}) %collective-permute-start.3) | collective-permute-done | bytes 36 | tf_op jit(solution)/shard_map/ppermute | solution.py:10
  594.4 0.6 collective-permute-start.5
  595.0 2.9 collective-permute-done.5
  598.1 1.0 sort.32
  599.1 1.9 constant_dynamic-update-slice_fusion.2
  601.0 1.9 constant_dynamic-update-slice_fusion.1
  602.8 1.9 constant_dynamic-update-slice_fusion
  604.7 2.3 gather_fusion.4
  607.0 1.5 copy.35
  608.5 1.9 copy.37
  (46 shorter events, 0.7 us)
Async XLA Ops:
  7.2 14.7 %copy-start.1 = (bf16[256,2560]{1,0:T(8,128)(2,1)S(1)}, bf16[256,2560]{1,0:T(8,128)(2,1)}, u32[]{:S(2)}) copy-start(bf16[256,2560]{1,0:T(8,128)(2,1)} %param.10) | copy-start | bytes 3932164
  7.2 14.7 %copy-start.3 = (f32[2560]{0:T(1024)S(1)}, f32[2560]{0:T(1024)}, u32[]{:S(2)}) copy-start(f32[2560]{0:T(1024)} %param.11) | copy-start | bytes 30724
  73.2 184.2 %copy-start.5 = (bf16[2,2560,384]{2,1,0:T(8,128)(2,1)S(1)}, bf16[2,2560,384]{2,1,0:T(8,128)(2,1)}, u32[]{:S(2)}) copy-start(bf16[2,2560,384]{2,1,0:T(8,128)(2,1)} %param.14) | copy-start | bytes 11796484
  254.3 3.2 copy-start
  322.8 5.3 copy-start.4
  322.8 179.5 %all-to-all-start.1 = ((bf16[2,776,2560]{2,0,1:T(2,128)(2,1)}), bf16[2,776,2560]{2,0,1:T(2,128)(2,1)}, u32[]{:S(2)}, u32[]{:S(2)}) async-start(bf16[2,776,2560]{2,0,1:T(2,128)(2,1)} %copy.28), calls=%async_computation.1 | async-start | bytes 15892480 | tf_op jit(solution)/shard_map/all_to_all | solution.py:103
  327.9 280.7 %reduce-scatter.4.cloned.1.call-start = ((), (), s32[]{:S(2)}) async-start(), calls=%async_computation.3 | async-start | bytes 1638400
  554.9 1.6 copy-start.6
  554.9 2.6 copy-start.7
  555.0 2.6 copy-start.2
  562.4 36.7 %collective-permute-start = (bf16[4,1,2,32,1024]{4,3,2,1,0:T(8,128)(2,1)}, bf16[4,1,2,32,1024]{4,3,2,1,0:T(8,128)(2,1)}, u32[]{:S(2)}, u32[]{:S(2)}) collective-permute-start(bf16[4,1,2,32,1024]{4,3,2,1,0:T(8,128)(2,1)} %get-tuple-element.12), channel_id=1, source_target_pairs={{24,0},{0,8},{8,16},{16,24},{25,1},{1,9},{9,17},{17,25},{26,2},{2,... | collective-permute-start | bytes 1572872 | tf_op jit(solution)/shard_map/ppermute | solution.py:10
  563.9 37.1 %collective-permute-start.1 = (bf16[4,1,2,32,1024]{4,3,2,1,0:T(8,128)(2,1)S(1)}, bf16[4,1,2,32,1024]{4,3,2,1,0:T(8,128)(2,1)}, u32[]{:S(2)}, u32[]{:S(2)}) collective-permute-start(bf16[4,1,2,32,1024]{4,3,2,1,0:T(8,128)(2,1)S(1)} %get-tuple-element.11), channel_id=1, source_target_pairs={{16,0},{24,8},{0,16},{8,24},{17,1},{25,9},{1,17},{9,25},{18,2},{26... | collective-permute-start | bytes 1572872 | tf_op jit(solution)/shard_map/ppermute | solution.py:10
  565.4 37.5 %collective-permute-start.2 = (bf16[4,1,2,32,1024]{4,3,2,1,0:T(8,128)(2,1)S(1)}, bf16[4,1,2,32,1024]{4,3,2,1,0:T(8,128)(2,1)}, u32[]{:S(2)}, u32[]{:S(2)}) collective-permute-start(bf16[4,1,2,32,1024]{4,3,2,1,0:T(8,128)(2,1)S(1)} %get-tuple-element.10), channel_id=1, source_target_pairs={{8,0},{16,8},{24,16},{0,24},{9,1},{17,9},{25,17},{1,25},{10,2},{18... | collective-permute-start | bytes 1572872 | tf_op jit(solution)/shard_map/ppermute | solution.py:10
  567.6 26.9 %collective-permute-start.3 = (bf16[1,1,2]{2,1,0:T(2,128)(2,1)S(1)}, bf16[1,1,2]{2,1,0:T(2,128)(2,1)S(1)}, u32[]{:S(2)}, u32[]{:S(2)}) collective-permute-start(bf16[1,1,2]{2,1,0:T(2,128)(2,1)S(1)} %get-tuple-element.15), channel_id=1, source_target_pairs={{24,0},{0,8},{8,16},{16,24},{25,1},{1,9},{9,17},{17,25},{26,2},{2,... | collective-permute-start | bytes 20 | tf_op jit(solution)/shard_map/ppermute | solution.py:10
  568.2 26.8 %collective-permute-start.4 = (bf16[1,1,2]{2,1,0:T(2,128)(2,1)S(1)}, bf16[1,1,2]{2,1,0:T(2,128)(2,1)S(1)}, u32[]{:S(2)}, u32[]{:S(2)}) collective-permute-start(bf16[1,1,2]{2,1,0:T(2,128)(2,1)S(1)} %get-tuple-element.14), channel_id=1, source_target_pairs={{16,0},{24,8},{0,16},{8,24},{17,1},{25,9},{1,17},{9,25},{18,2},{26... | collective-permute-start | bytes 20 | tf_op jit(solution)/shard_map/ppermute | solution.py:10
  594.4 3.5 collective-permute-start.5
Sparse Core Ops, SparseCore 0:
  556.6 44.8 reduce-scatter.3
where the time goes:
time: 618 us; the launch traced here: 617 us
  waiting for transfers between devices  201 us (33%)
  blocking collectives  181 us (29%)
  local copies, waits for them, and re-layouts  166 us (27%)
  other arithmetic  21.9 us (4%)
  matrix products  21.7 us (4%)
  between operations  14.4 us (2%)
  starting transfers between devices  11.5 us (2%)
    all_to_all x1, blocking collectives, per_device(): lax.all_to_all(outgoing, 'exp', split_axis=1, concat_axis=1, tiled=True)  181 us
    all_to_all x1, waiting for transfers between devices, per_device(): lax.all_to_all(partial_value, 'exp', split_axis=1, concat_axis=1, tiled=T...  174 us
    convert_element_type x1, local copies, waits for them, and re-layouts, expert_block(): jnp.einsum('erf,efd->erd', hidden, w_down, preferred_element_type=jnp.flo...  43.6 us
    reshape x1, local copies, waits for them, and re-layouts, per_device(): fill_slots(normed, slot_index, total_slots, topk)  42.7 us
    ppermute x6, waiting for transfers between devices, passed_along(): return lax.ppermute(block, axis, route)  27.1 us
    gather x1, local copies, waits for them, and re-layouts, per_device(): returned[slot_index].astype(jnp.float32).reshape(tok_count, topk, width)  19.4 us
    dot_general x1, matrix products, expert_block(): jnp.einsum('erf,efd->erd', hidden, w_down, preferred_element_type=jnp.flo...  16 us
    convert_element_type x1, local copies, waits for them, and re-layouts, per_device(): returned[slot_index].astype(jnp.float32).reshape(tok_count, topk, width)  14.2 us
  transfers between devices with their start and end apart: 8, of which 3 were waited for; matrix products, arithmetic and copies ran while one was open for 3% of the time, Pallas kernels for 0%

commit v1 on v0

v1 whole, which is shorter than its diff:
```python
import jax
import jax.numpy as jnp
from jax import lax
from jax.experimental import pallas as pl
from jax.experimental.pallas import tpu as pltpu
from jax.sharding import PartitionSpec as P

LANES = 128


def passed_along(block, axis, distance):
    devices = range(lax.axis_size(axis))
    route = [((i - distance) % len(devices), i) for i in devices]
    return lax.ppermute(block, axis, route)


def rms_normed(tokens, norm_gain):
    values = tokens.astype(jnp.float32)
    scale = lax.rsqrt(jnp.mean(values * values, axis=-1, keepdims=True) + 1e-06)
    return (values * scale * norm_gain).astype(jnp.bfloat16)


def coefficients(routes, route_weights, experts):
    width = -(-experts // LANES) * LANES
    lane = jnp.arange(width, dtype=jnp.int32)
    chosen = routes[:, :, None] == lane[None, None, :]
    weights = route_weights.astype(jnp.float32)[:, :, None]
    return jnp.sum(jnp.where(chosen, weights, 0.0), axis=1).astype(jnp.bfloat16)


def placed(source, where, value):
    spot = jnp.arange(source, dtype=jnp.int32)
    hit = where[None, :] == spot[:, None]
    return jnp.sum(jnp.where(hit, value[None, :], 0), axis=1)


def sorted_order(key):
    rank = jnp.sum((key[None, :] < key[:, None]).astype(jnp.int32), axis=1)
    return rank


def pick_kernel(order_ref, empty_ref, block_ref, out_ref):
    i = pl.program_id(0)
    empty = empty_ref[order_ref[i]]
    out_ref[...] = jnp.where(empty == 1, jnp.zeros_like(block_ref[...]), block_ref[...]).reshape(
        out_ref.shape
    )


def pick_blocks(kv_prefill, order, block_empty):
    layers, blocks, block_rows, kv_width = kv_prefill.shape
    return pl.pallas_call(
        pick_kernel,
        out_shape=jax.ShapeDtypeStruct((blocks, layers, block_rows, kv_width), kv_prefill.dtype),
        grid_spec=pltpu.PrefetchScalarGridSpec(
            num_scalar_prefetch=2,
            grid=(blocks,),
            in_specs=[
                pl.BlockSpec((layers, 1, block_rows, kv_width), lambda i, o, e: (0, o[i], 0, 0))
            ],
            out_specs=pl.BlockSpec(
                (1, layers, block_rows, kv_width), lambda i, o, e: (i, 0, 0, 0)
            ),
        ),
    )(order, block_empty, kv_prefill)


def put_kernel(slot_ref, block_ref, out_ref):
    out_ref[...] = block_ref[...].reshape(out_ref.shape)


def put_blocks(arrived, slots):
    blocks, layers, block_rows, kv_width = arrived.shape
    return pl.pallas_call(
        put_kernel,
        out_shape=jax.ShapeDtypeStruct((layers, blocks, block_rows, kv_width), arrived.dtype),
        grid_spec=pltpu.PrefetchScalarGridSpec(
            num_scalar_prefetch=1,
            grid=(blocks,),
            in_specs=[
                pl.BlockSpec((1, layers, block_rows, kv_width), lambda i, s: (i, 0, 0, 0))
            ],
            out_specs=pl.BlockSpec(
                (layers, 1, block_rows, kv_width), lambda i, s: (0, s[i], 0, 0)
            ),
        ),
    )(slots, arrived)


def outgoing_blocks(kv_prefill, block_map, block_empty):
    blocks = kv_prefill.shape[1]
    exp_count = lax.axis_size("exp")
    place = jnp.arange(blocks, dtype=jnp.int32)
    peer = block_map // blocks // exp_count
    rank = sorted_order(peer * blocks + place)
    order = placed(blocks, rank, place)
    targets = placed(blocks, rank, block_map % blocks)
    return pick_blocks(kv_prefill, order, block_empty), targets


def relayout(kv_prefill, block_map, block_empty):
    blocks = kv_prefill.shape[1]
    seq_count = lax.axis_size("seq")
    per_peer = blocks // seq_count
    outgoing, targets = outgoing_blocks(kv_prefill, block_map, block_empty)
    my_seq = lax.axis_index("seq")
    arrived, tags = outgoing, targets
    for step in range(1, seq_count):
        ahead = (my_seq + step) % seq_count
        piece = lax.dynamic_slice_in_dim(outgoing, ahead * per_peer, per_peer, 0)
        label = lax.dynamic_slice_in_dim(targets, ahead * per_peer, per_peer, 0)
        piece, label = passed_along((piece, label), "seq", step)
        behind = (my_seq - step + seq_count) % seq_count
        arrived = lax.dynamic_update_slice_in_dim(arrived, piece, behind * per_peer, 0)
        tags = lax.dynamic_update_slice_in_dim(tags, label, behind * per_peer, 0)
    return put_blocks(arrived, tags)


def dense_experts(rows, coef, w_gate, w_up, w_down):
    total = None
    for e in range(w_gate.shape[0]):
        gate = jnp.dot(rows, w_gate[e], preferred_element_type=jnp.float32)
        upward = jnp.dot(rows, w_up[e], preferred_element_type=jnp.float32)
        hidden = jax.nn.silu(gate) * upward * coef[:, e : e + 1].astype(jnp.float32)
        part = jnp.dot(
            hidden.astype(jnp.bfloat16), w_down[e], preferred_element_type=jnp.float32
        )
        total = part if total is None else total + part
    return total.astype(jnp.bfloat16)


def plain(packed, w_gate, w_up, w_down):
    width = w_gate.shape[1]
    local_experts = w_gate.shape[0]
    everyone = lax.all_gather(packed, "exp", axis=0, tiled=True)
    rows = everyone[:, :width]
    coef = lax.dynamic_slice_in_dim(
        everyone[:, width:], lax.axis_index("exp") * local_experts, local_experts, 1
    )
    partial_value = dense_experts(rows, coef, w_gate, w_up, w_down)
    held = lax.psum_scatter(partial_value, "seq", scatter_dimension=1, tiled=True)
    return lax.psum_scatter(held, "exp", scatter_dimension=0, tiled=True)


def per_device(
    tokens,
    norm_gain,
    routes,
    route_weights,
    w_gate,
    w_up,
    w_down,
    kv_prefill,
    block_map,
    block_empty,
):
    experts = w_gate.shape[0] * lax.axis_size("exp")
    normed = rms_normed(tokens, norm_gain)
    packed = jnp.concatenate([normed, coefficients(routes, route_weights, experts)], axis=1)
    half = packed.shape[0] // 2
    mixed = jnp.concatenate(
        [plain(packed[i : i + half], w_gate, w_up, w_down) for i in (0, half)], axis=0
    )
    kv_decode = relayout(kv_prefill, block_map, block_empty)
    return (mixed, kv_decode)


def solution(mesh):
    in_specs = (
        P("exp", None),
        P(),
        P("exp", None),
        P("exp", None),
        P("exp", None, "seq"),
        P("exp", None, "seq"),
        P("exp", "seq", None),
        P(None, ("seq", "exp"), None, None),
        P(("seq", "exp")),
        P(("seq", "exp")),
    )
    out_specs = (P("exp", "seq"), P(None, ("seq", "exp"), None, None))
    return jax.shard_map(
        per_device, mesh=mesh, in_specs=in_specs, out_specs=out_specs, check_vma=False
    )
```

time: 618 us -> 377 us (0.61)
  blocking collectives: 181 us -> 0 us
  local copies, waits for them, and re-layouts: 166 us -> 28.4 us
  matrix products: 21.7 us -> 65.7 us
  waiting for transfers between devices: 201 us -> 239 us
  other arithmetic: 21.9 us -> 8.54 us
  Pallas kernels: 0 us -> 12.7 us
    all_to_all x1 -> x0, blocking collectives: 181 us -> none  [per_device(): lax.all_to_all(outgoing, 'exp', split_axis=1, concat_axis=1, tiled=True)]
    all_to_all x1 -> x0, waiting for transfers between devices: 174 us -> none  [per_device(): lax.all_to_all(partial_value, 'exp', split_axis=1, concat_axis=1, tiled=T...]
    all_gather x0 -> x2, waiting for transfers between devices: none -> 118 us  [plain(): everyone = lax.all_gather(packed, 'exp', axis=0, tiled=True)]
    unnamed x2 -> x8, waiting for transfers between devices: 0.02 us -> 80.5 us
    convert_element_type x5 -> x0, local copies, waits for them, and re-layouts: 58.2 us -> none  [the longest x1 43.6 us: expert_block(): jnp.einsum('erf,efd->erd', hidden, w_down, preferred_element_type=jnp.flo...]
    reshape x3 -> x0, local copies, waits for them, and re-layouts: 44.4 us -> none  [the longest x1 42.7 us: per_device(): fill_slots(normed, slot_index, total_slots, topk)]
    dot_general x2 -> x8, matrix products: 21.7 us -> 65.7 us  [the longest x4 46.7 us: dense_experts(): jnp.dot(hidden.astype(jnp.bfloat16), w_down[e], preferred_element_type=jn...]
    gather x5 -> x0, local copies, waits for them, and re-layouts: 32.7 us -> none  [the longest x1 19.4 us: per_device(): returned[slot_index].astype(jnp.float32).reshape(tok_count, topk, width)]
  transfers between devices with their start and end apart: 8 -> 12, of which waited for: 3 -> 7; matrix products, arithmetic and copies ran while one was open for 3% -> 14% of each run, Pallas kernels for 0% -> 3%
where the time goes in v1:
time: 377 us; the launch traced here: 376 us
  waiting for transfers between devices  239 us (63%)
  matrix products  65.7 us (17%)
  local copies, waits for them, and re-layouts  28.4 us (8%)
  between operations  14.3 us (4%)
  Pallas kernels  12.7 us (3%)
  other arithmetic  8.54 us (2%)
  starting transfers between devices  7.35 us (2%)
    all_gather x2, waiting for transfers between devices, plain(): everyone = lax.all_gather(packed, 'exp', axis=0, tiled=True)  118 us
    unnamed x8, waiting for transfers between devices  80.5 us
    dot_general x4, matrix products, dense_experts(): jnp.dot(hidden.astype(jnp.bfloat16), w_down[e], preferred_element_type=jn...  46.7 us
    ppermute x6, waiting for transfers between devices, passed_along(): return lax.ppermute(block, axis, route)  21.6 us
    unnamed x20, local copies, waits for them, and re-layouts  20.8 us
    dot_general x4, matrix products, dense_experts(): gate = jnp.dot(rows, w_gate[e], preferred_element_type=jnp.float32)  19 us
    reduce_scatter x2, waiting for transfers between devices, plain(): return lax.psum_scatter(held, 'exp', scatter_dimension=0, tiled=True)  18.9 us
  transfers between devices with their start and end apart: 12, of which 7 were waited for; matrix products, arithmetic and copies ran while one was open for 14% of the time, Pallas kernels for 3%

profile of v1, /device:TPU:0, one launch (start us, length us, event | category | flops | bytes accessed | tf_op | source)
XLA Modules:
  0.0 376.0 jit_solution(8767163214098441193)
XLA Ops:
  7.2 1.7 fusion.16
  9.0 0.7 convert_element_type.39
  9.7 1.1 fusion.18
  10.8 0.6 select_reduce_fusion
  11.3 1.2 fusion.85
  12.6 0.7 all-gather.5.cloned.1.call-update
  13.3 60.3 %all-gather.3.cloned.1.call-done = bf16[1024,2688]{1,0:T(8,128)(2,1)} async-done(((bf16[128,2688]{1,0:T(8,128)(2,1)}), bf16[1024,2688]{1,0:T(8,128)(2,1)}) %all-gather.3.cloned.1.call-update) | async-done | bytes 5505040 | tf_op jit(solution)/shard_map/all_gather | solution.py:135
  73.6 1.0 slice.73
  74.6 57.7 %all-gather.5.cloned.1.call-done = bf16[1024,2688]{1,0:T(8,128)(2,1)} async-done(((bf16[128,2688]{1,0:T(8,128)(2,1)}), bf16[1024,2688]{1,0:T(8,128)(2,1)}) %all-gather.5.cloned.1.call-update) | async-done | bytes 5505040 | tf_op jit(solution)/shard_map/all_gather | solution.py:135
  132.3 1.0 slice.75
  133.2 0.7 convert_reduce_fusion
  134.0 5.8 %fusion.14 = f32[1024,384]{1,0:T(8,128)S(1)} fusion(bf16[1024,2688]{1,0:T(8,128)(2,1)} %all-gather.3.cloned.1.call-done, bf16[2,2560,384]{2,1,0:T(8,128)(2,1)} %param.14), kind=kOutput, calls=%fused_computation.16 | convolution fusion | flops 2013265920 | bytes 8781824 | tf_op jit(solution)/shard_map/dot_general | solution.py:122
  139.8 2.9 fusion.10
  142.6 11.2 %fusion.27 = f32[1024,2560]{1,0:T(8,128)} fusion(bf16[2,384,2560]{2,1,0:T(8,128)(2,1)} %param.16, f32[1024,384]{1,0:T(8,128)S(1)} %fusion.14, bf16[2,2560,384]{2,1,0:T(8,128)(2,1)} %param.15, bf16[1024,2688]{1,0:T(8,128)(2,1)} %all-gather.3.cloned.1.call-done, f32[1024]{0:T(1024)S(1)} %get-tuple-element.18), kind=kOutput, calls=%fused_computation.31 | convolution fusion | flops 4029284352 | bytes 21237760 | tf_op jit(solution)/shard_map/dot_general | solution.py:125
  153.8 11.9 %add_convert_fusion.1 = bf16[1024,2560]{1,0:T(8,128)(2,1)} fusion(f32[1024,2560]{1,0:T(8,128)} %fusion.27, bf16[2,384,2560]{2,1,0:T(8,128)(2,1)} %param.16, f32[1024,384]{1,0:T(8,128)S(1)} %fusion.10, bf16[2,2560,384]{2,1,0:T(8,128)(2,1)} %param.15, bf16[1024,2688]{1,0:T(8,128)(2,1)} %all-gather.3.cloned.1.call-done, f32[1024]{0:T(1024)S(1)} %get-tuple-element.19), kind=kOutput, calls=%fused_computation.1 | convolution fusion | flops 4034527232 | bytes 26480640 | tf_op jit(solution)/shard_map/dot_general | solution.py:125
  165.7 8.0 %copy.18 = bf16[1024,2560]{0,1:T(8,128)(2,1)} copy(bf16[1024,2560]{1,0:T(8,128)(2,1)} %add_convert_fusion.1) | data formatting | bytes 10485760
  173.6 0.2 reduce-scatter.15.cloned.1.call-start
  173.9 5.5 %fusion.6 = f32[1024,384]{1,0:T(8,128)S(1)} fusion(bf16[1024,2688]{1,0:T(8,128)(2,1)} %all-gather.5.cloned.1.call-done, bf16[2,2560,384]{2,1,0:T(8,128)(2,1)} %param.14), kind=kOutput, calls=%fused_computation.8 | convolution fusion | flops 2013265920 | bytes 8781824 | tf_op jit(solution)/shard_map/dot_general | solution.py:122
  179.4 4.8 %fusion.2 = f32[1024,384]{1,0:T(8,128)S(1)} fusion(bf16[1024,2688]{1,0:T(8,128)(2,1)} %all-gather.5.cloned.1.call-done, bf16[2,2560,384]{2,1,0:T(8,128)(2,1)S(1)} %copy-done.4), kind=kOutput, calls=%fused_computation.4 | convolution fusion | flops 2013265920 | bytes 8781824 | tf_op jit(solution)/shard_map/dot_general | solution.py:122
  184.3 11.5 %fusion.25 = f32[1024,2560]{1,0:T(8,128)} fusion(bf16[2,384,2560]{2,1,0:T(8,128)(2,1)} %param.16, f32[1024,384]{1,0:T(8,128)S(1)} %fusion.6, bf16[2,2560,384]{2,1,0:T(8,128)(2,1)} %param.15, bf16[1024,2688]{1,0:T(8,128)(2,1)} %all-gather.5.cloned.1.call-done, f32[1024]{0:T(1024)S(1)} %get-tuple-element.5), kind=kOutput, calls=%fused_computation.29 | convolution fusion | flops 4029284352 | bytes 21237760 | tf_op jit(solution)/shard_map/dot_general | solution.py:125
  195.8 12.2 %add_convert_fusion = bf16[1024,2560]{1,0:T(8,128)(2,1)} fusion(f32[1024,2560]{1,0:T(8,128)} %fusion.25, bf16[2,384,2560]{2,1,0:T(8,128)(2,1)} %param.16, f32[1024,384]{1,0:T(8,128)S(1)} %fusion.2, bf16[2,2560,384]{2,1,0:T(8,128)(2,1)} %param.15, bf16[1024,2688]{1,0:T(8,128)(2,1)} %all-gather.5.cloned.1.call-done, f32[1024]{0:T(1024)S(1)} %get-tuple-element.4), kind=kOutput, calls=%fused_computation | convolution fusion | flops 4034527232 | bytes 26480640 | tf_op jit(solution)/shard_map/dot_general | solution.py:125
  208.0 8.0 %copy.20 = bf16[1024,2560]{0,1:T(8,128)(2,1)} copy(bf16[1024,2560]{1,0:T(8,128)(2,1)} %add_convert_fusion) | data formatting | bytes 10485760
  216.0 17.9 %reduce-scatter.13.cloned.1.call-done = bf16[640,1024]{1,0:T(8,128)(2,1)} async-done(((bf16[2560,1024]{1,0:T(8,128)(2,1)}), bf16[640,1024]{1,0:T(8,128)(2,1)}) %reduce-scatter.13.cloned.1.call-update) | async-done | bytes 1310736
  234.0 2.4 copy.19
  236.5 61.8 %reduce-scatter.15.cloned.1.call-done = bf16[640,1024]{1,0:T(8,128)(2,1)} async-done(((bf16[2560,1024]{1,0:T(8,128)(2,1)}), bf16[640,1024]{1,0:T(8,128)(2,1)}) %reduce-scatter.15.cloned.1.call-update) | async-done | bytes 1310736
  298.3 2.4 copy.21
  300.8 0.2 convert_reduce_fusion.4
  301.0 0.6 select_reduce_fusion.1
  301.6 6.4 %shard_map.113 = bf16[8,4,32,1024]{3,2,1,0:T(8,128)(2,1)} custom-call(s32[8]{0:T(128)} %get-tuple-element.6.order_ref, s32[8]{0:T(128)} %empty_ref.1, bf16[4,8,32,1024]{3,2,1,0:T(8,128)(2,1)} %block_ref.1), custom_call_target="tpu_custom_call" | custom-call | tf_op jit(solution)/shard_map/pallas_call | solution.py:52
  308.0 1.1 constant_dynamic-slice_fusion.2
  309.1 1.4 collective-permute-start.3
  310.5 13.2 %collective-permute-done.3 = bf16[2,4,32,1024]{3,2,1,0:T(8,128)(2,1)S(1)} collective-permute-done((bf16[2,4,32,1024]{3,2,1,0:T(8,128)(2,1)S(1)}, bf16[2,4,32,1024]{3,2,1,0:T(8,128)(2,1)S(1)}, u32[]{:S(2)}, u32[]{:S(2)}) %collective-permute-start.3) | collective-permute-done | bytes 524320 | tf_op jit(solution)/shard_map/ppermute | solution.py:14
  323.7 2.1 constant_dynamic-slice_fusion
  325.9 1.3 collective-permute-start.4
  327.2 0.6 collective-permute-start.5
  327.7 0.1 fusion.90
  327.8 1.5 collective-permute-start
  329.3 0.7 collective-permute-start.1
  330.0 1.5 collective-permute-start.2
  331.5 8.4 %collective-permute-done = s32[2]{0:T(128)S(1)} collective-permute-done((s32[2]{0:T(128)S(1)}, s32[2]{0:T(128)S(1)}, u32[]{:S(2)}, u32[]{:S(2)}) %collective-permute-start) | collective-permute-done | bytes 40 | tf_op jit(solution)/shard_map/ppermute | solution.py:14
  339.9 0.2 dynamic_update_slice.18
  340.0 0.2 dynamic_update_slice.19
  340.3 0.2 dynamic_update_slice.20.slot_ref
  340.5 0.9 constant_dynamic-update-slice_fusion.1
  341.3 0.8 constant_dynamic-update-slice_fusion.block_ref
  342.2 6.3 %shard_map.114 = bf16[4,8,32,1024]{3,2,1,0:T(8,128)(2,1)} custom-call(s32[8]{0:T(128)} %copy-done.1, bf16[8,4,32,1024]{3,2,1,0:T(8,128)(2,1)} %constant_dynamic-update-slice_fusion.block_ref), custom_call_target="tpu_custom_call" | custom-call | tf_op jit(solution)/shard_map/pallas_call | solution.py:74
  348.5 18.9 %reduce-scatter.11.cloned.1.call-done = bf16[128,640]{1,0:T(8,128)(2,1)} async-done(((bf16[1024,640]{1,0:T(8,128)(2,1)}), bf16[128,640]{1,0:T(8,128)(2,1)}) %reduce-scatter.11.cloned.1.call-update) | async-done | bytes 163856 | tf_op jit(solution)/shard_map/reduce_scatter | solution.py:142
  367.4 1.7 pad_maximum_fusion.1
  (34 shorter events, 0.4 us)
Async XLA Ops:
  7.2 2.5 copy-start
  7.2 3.6 copy-start.2
  7.2 66.4 %all-gather.3.cloned.1.call-start = ((), (), s32[]{:S(2)}) async-start(), calls=%async_computation.4 | async-start | bytes 6193152 | tf_op jit(solution)/shard_map/all_gather | solution.py:135
  12.5 119.7 %all-gather.5.cloned.1.call-start = ((), (), s32[]{:S(2)}) async-start(), calls=%async_computation.6 | async-start | bytes 6193152 | tf_op jit(solution)/shard_map/all_gather | solution.py:135
  13.3 220.7 %reduce-scatter.13.cloned.1.call-start = ((), (), s32[]{:S(2)}) async-start(), calls=%async_computation.8 | async-start | bytes 6553600
  133.2 6.5 %slice-start = ((s8[5505024]{0:T(1024)(128)(4,1)}), s8[4194304]{0:T(1024)(128)(4,1)S(1)}, s32[]{:S(2)}) async-start(s8[5505024]{0:T(1024)(128)(4,1)} %bitcast.54), calls=%async_computation.10 | async-start | bytes 8388608
  133.9 5.8 %slice-start.1 = ((s8[5505024]{0:T(1024)(128)(4,1)}), s8[1310720]{0:T(1024)(128)(4,1)S(1)}, s32[]{:S(2)}) async-start(s8[5505024]{0:T(1024)(128)(4,1)} %bitcast.54), calls=%async_computation.11 | async-start | bytes 2621440
  134.0 5.8 %copy-start.3 = (bf16[2,2560,384]{2,1,0:T(8,128)(2,1)S(1)}, bf16[2,2560,384]{2,1,0:T(8,128)(2,1)}, u32[]{:S(2)}) copy-start(bf16[2,2560,384]{2,1,0:T(8,128)(2,1)} %param.14) | copy-start | bytes 11796484
  173.6 124.6 %reduce-scatter.15.cloned.1.call-start = ((), (), s32[]{:S(2)}) async-start(), calls=%async_computation.9 | async-start | bytes 6553600
  173.9 5.6 %copy-start.4 = (bf16[2,2560,384]{2,1,0:T(8,128)(2,1)S(1)}, bf16[2,2560,384]{2,1,0:T(8,128)(2,1)}, u32[]{:S(2)}) copy-start(bf16[2,2560,384]{2,1,0:T(8,128)(2,1)} %param.14) | copy-start | bytes 11796484
  216.0 132.5 %reduce-scatter.9.cloned.1.call-start = ((), (), s32[]{:S(2)}) async-start(), calls=%async_computation.5 | async-start | bytes 1474560 | tf_op jit(solution)/shard_map/reduce_scatter | solution.py:142
  236.4 64.3 %copy-start.5 = (s32[8]{0:T(128)S(1)}, s32[8]{0:T(128)}, u32[]{:S(2)}) copy-start(s32[8]{0:T(128)} %param.18) | copy-start | bytes 100
  236.5 130.9 %reduce-scatter.11.cloned.1.call-start = ((), (), s32[]{:S(2)}) async-start(), calls=%async_computation.7 | async-start | bytes 1474560 | tf_op jit(solution)/shard_map/reduce_scatter | solution.py:142
  309.1 14.6 %collective-permute-start.3 = (bf16[2,4,32,1024]{3,2,1,0:T(8,128)(2,1)S(1)}, bf16[2,4,32,1024]{3,2,1,0:T(8,128)(2,1)S(1)}, u32[]{:S(2)}, u32[]{:S(2)}) collective-permute-start(bf16[2,4,32,1024]{3,2,1,0:T(8,128)(2,1)S(1)} %constant_dynamic-slice_fusion.2), channel_id=1, source_target_pairs={{24,0},{0,8},{8,16},{16,24},{25,1},{1,9},{9,17},{17,25},{26,2},{2,... | collective-permute-start | bytes 1572872 | tf_op jit(solution)/shard_map/ppermute | solution.py:14
  325.9 14.6 %collective-permute-start.4 = (bf16[2,4,32,1024]{3,2,1,0:T(8,128)(2,1)S(1)}, bf16[2,4,32,1024]{3,2,1,0:T(8,128)(2,1)S(1)}, u32[]{:S(2)}, u32[]{:S(2)}) collective-permute-start(bf16[2,4,32,1024]{3,2,1,0:T(8,128)(2,1)S(1)} %get-tuple-element.9), channel_id=1, source_target_pairs={{16,0},{24,8},{0,16},{8,24},{17,1},{25,9},{1,17},{9,25},{18,2},{26... | collective-permute-start | bytes 1572872 | tf_op jit(solution)/shard_map/ppermute | solution.py:14
  327.2 14.1 %collective-permute-start.5 = (bf16[2,4,32,1024]{3,2,1,0:T(8,128)(2,1)S(1)}, bf16[2,4,32,1024]{3,2,1,0:T(8,128)(2,1)S(1)}, u32[]{:S(2)}, u32[]{:S(2)}) collective-permute-start(bf16[2,4,32,1024]{3,2,1,0:T(8,128)(2,1)S(1)} %get-tuple-element.8), channel_id=1, source_target_pairs={{8,0},{16,8},{24,16},{0,24},{9,1},{17,9},{25,17},{1,25},{10,2},{18... | collective-permute-start | bytes 1572872 | tf_op jit(solution)/shard_map/ppermute | solution.py:14
  327.8 12.0 %collective-permute-start = (s32[2]{0:T(128)S(1)}, s32[2]{0:T(128)S(1)}, u32[]{:S(2)}, u32[]{:S(2)}) collective-permute-start(s32[2]{0:T(128)S(1)} %get-tuple-element.15), channel_id=1, source_target_pairs={{24,0},{0,8},{8,16},{16,24},{25,1},{1,9},{9,17},{17,25},{26,2},{2,... | collective-permute-start | bytes 32 | tf_op jit(solution)/shard_map/ppermute | solution.py:14
  329.3 10.7 %collective-permute-start.1 = (s32[2]{0:T(128)S(1)}, s32[2]{0:T(128)S(1)}, u32[]{:S(2)}, u32[]{:S(2)}) collective-permute-start(s32[2]{0:T(128)S(1)} %get-tuple-element.14), channel_id=1, source_target_pairs={{16,0},{24,8},{0,16},{8,24},{17,1},{25,9},{1,17},{9,25},{18,2},{26... | collective-permute-start | bytes 32 | tf_op jit(solution)/shard_map/ppermute | solution.py:14
  330.0 10.3 %collective-permute-start.2 = (s32[2]{0:T(128)S(1)}, s32[2]{0:T(128)S(1)}, u32[]{:S(2)}, u32[]{:S(2)}) collective-permute-start(s32[2]{0:T(128)S(1)} %get-tuple-element.13), channel_id=1, source_target_pairs={{8,0},{16,8},{24,16},{0,24},{9,1},{17,9},{25,17},{1,25},{10,2},{18... | collective-permute-start | bytes 32 | tf_op jit(solution)/shard_map/ppermute | solution.py:14
  340.5 1.7 copy-start.1
Sparse Core Ops, SparseCore 0:
  12.7 60.9 all-gather.2
  75.3 56.9 all-gather.4
  173.8 60.1 reduce-scatter.12
  236.8 61.4 reduce-scatter.14
  300.4 33.3 reduce-scatter.8
  335.9 31.4 reduce-scatter.10

commit v2 on v1

--- a/solution.py
+++ b/solution.py
@@ -142,6 +142,355 @@
     return lax.psum_scatter(held, "exp", scatter_dimension=0, tiled=True)
 
 
+def fused_kernel(
+    packed_ref,
+    w_gate_ref,
+    w_up_ref,
+    w_down_ref,
+    kv_ref,
+    label_ref,
+    out_ref,
+    arrived_ref,
+    tag_ref,
+    held,
+    gate_w,
+    up_w,
+    down_w,
+    hidden,
+    part,
+    pair,
+    slices,
+    summed,
+    columns,
+    local_sem,
+    z_send,
+    z_recv,
+    row_send,
+    row_recv,
+    core_send,
+    core_recv,
+    pair_send,
+    pair_recv,
+    slice_send,
+    slice_recv,
+    sum_send,
+    sum_recv,
+    kv_send,
+    kv_recv,
+    label_send,
+    label_recv,
+):
+    local_experts, width, ff = w_gate_ref.shape
+    n_z, n_seq = slices.shape[0], slices.shape[1]
+    tokens = packed_ref.shape[0]
+    quarter = tokens // n_seq
+    per_peer = kv_ref.shape[0] // n_seq
+    seq = lax.axis_index("seq")
+    me = lax.axis_index("exp")
+    z, core = me // 2, lax.rem(me, 2)
+
+    def remote(src, dst, send, recv, to_seq, to_exp):
+        return pltpu.make_async_remote_copy(
+            src_ref=src,
+            dst_ref=dst,
+            send_sem=send,
+            recv_sem=recv,
+            device_id={"seq": to_seq, "exp": to_exp},
+            device_id_type=pl.DeviceIdType.MESH,
+        )
+
+    loads = []
+    for e in range(local_experts):
+        spot = pl.ds(e * ff, ff)
+        loads.append((w_gate_ref.at[e], gate_w.at[:, spot]))
+        loads.append((w_up_ref.at[e], up_w.at[:, spot]))
+        loads.append((w_down_ref.at[e], down_w.at[spot]))
+    mine = pl.ds(seq * per_peer, per_peer)
+    loads.append((kv_ref.at[mine], arrived_ref.at[mine]))
+    loads.append((label_ref.at[seq], tag_ref.at[seq]))
+    loads = [pltpu.make_async_copy(a, b, local_sem.at[i]) for i, (a, b) in enumerate(loads)]
+    for load in loads:
+        load.start()
+
+    def other_z(d):
+        return lax.rem(z + d, n_z)
+
+    def other_seq(d):
+        return lax.rem(seq + d, n_seq)
+
+    sibling = z * 2 + 1 - core
+    barrier = pltpu.get_barrier_semaphore()
+    pl.semaphore_signal(
+        barrier, 1, device_id={"seq": seq, "exp": sibling}, device_id_type=pl.DeviceIdType.MESH
+    )
+    for d in range(1, n_z):
+        pl.semaphore_signal(
+            barrier,
+            1,
+            device_id={"seq": seq, "exp": other_z(d) * 2 + core},
+            device_id_type=pl.DeviceIdType.MESH,
+        )
+    for d in range(1, n_seq):
+        pl.semaphore_signal(
+            barrier,
+            1,
+            device_id={"seq": other_seq(d), "exp": me},
+            device_id_type=pl.DeviceIdType.MESH,
+        )
+    held[me] = packed_ref[...]
+    pl.semaphore_wait(barrier, n_z + n_seq - 1)
+
+    own_rows = pl.ds(seq * quarter, quarter)
+
+    def to_z(d):
+        rows = held.at[me, own_rows]
+        return remote(rows, rows, z_send.at[d], z_recv.at[z], seq, other_z(d) * 2 + core)
+
+    def from_z(zs):
+        rows = held.at[zs * 2 + core, own_rows]
+        return remote(rows, rows, z_send.at[0], z_recv.at[zs], seq, sibling)
+
+    def to_row(zs, d):
+        rows = held.at[zs * 2 + core, own_rows]
+        return remote(
+            rows, rows, row_send.at[zs, d], row_recv.at[zs, seq], other_seq(d), me
+        )
+
+    def from_row(zs, peer):
+        rows = held.at[zs * 2 + core, pl.ds(peer * quarter, quarter)]
+        return remote(rows, rows, row_send.at[0, 0], row_recv.at[zs, peer], seq, sibling)
+
+    def to_core(zs):
+        block = held.at[zs * 2 + core]
+        return remote(block, block, core_send.at[zs], core_recv.at[zs], seq, sibling)
+
+    def from_core(zs):
+        block = held.at[zs * 2 + 1 - core]
+        return remote(block, block, core_send.at[0], core_recv.at[zs], seq, sibling)
+
+    def to_pair(zs):
+        return remote(part.at[1, zs], pair.at[zs], pair_send.at[zs], pair_recv.at[zs], seq, sibling)
+
+    def to_slice(zs, d):
+        peer = other_seq(d)
+        return remote(
+            part.at[0, zs, peer],
+            slices.at[zs, seq],
+            slice_send.at[zs, d],
+            slice_recv.at[zs, seq],
+            peer,
+            me,
+        )
+
+    def from_slice(zs, peer):
+        spot = slices.at[zs, peer]
+        return remote(spot, spot, slice_send.at[0, 0], slice_recv.at[zs, peer], seq, sibling)
+
+    def to_sum(zs):
+        return remote(
+            summed.at[zs], columns.at[z], sum_send.at[zs], sum_recv.at[z], seq, zs * 2 + core
+        )
+
+    def from_sum(zs):
+        spot = columns.at[zs]
+        return remote(spot, spot, sum_send.at[0], sum_recv.at[zs], seq, sibling)
+
+    def to_kv(d):
+        peer = other_seq(d)
+        return remote(
+            kv_ref.at[pl.ds(peer * per_peer, per_peer)],
+            arrived_ref.at[mine],
+            kv_send.at[d],
+            kv_recv.at[seq],
+            peer,
+            me,
+        )
+
+    def from_kv(peer):
+        spot = arrived_ref.at[pl.ds(peer * per_peer, per_peer)]
+        return remote(spot, spot, kv_send.at[0], kv_recv.at[peer], seq, sibling)
+
+    def to_label(d):
+        peer = other_seq(d)
+        return remote(
+            label_ref.at[peer], tag_ref.at[seq], label_send.at[d], label_recv.at[seq], peer, me
+        )
+
+    def from_label(peer):
+        spot = tag_ref.at[peer]
+        return remote(spot, spot, label_send.at[0], label_recv.at[peer], seq, sibling)
+
+    for d in range(1, n_z):
+        to_z(d).start()
+    to_core(z).start()
+    for d in range(1, n_seq):
+        to_kv(d).start()
+        to_label(d).start()
+    for load in loads:
+        load.wait()
+
+    def compute(block, j, zs):
+        rows = held[block, :, :width]
+        coef = held[block, :, width:].astype(jnp.float32)
+        lane = lax.broadcasted_iota(jnp.int32, coef.shape, 1)
+        gate = jnp.dot(rows, gate_w[...], preferred_element_type=jnp.float32)
+        upward = jnp.dot(rows, up_w[...], preferred_element_type=jnp.float32)
+        value = gate / (1.0 + jnp.exp(-gate)) * upward
+        for e in range(local_experts):
+            scale = jnp.sum(
+                jnp.where(lane == me * local_experts + e, coef, 0.0), axis=1, keepdims=True
+            )
+            spot = slice(e * ff, (e + 1) * ff)
+            hidden[:, spot] = (value[:, spot] * scale).astype(hidden.dtype)
+        out_width = part.shape[-1]
+        for s in range(n_seq):
+            down = down_w[:, s * out_width : (s + 1) * out_width]
+            part[j, zs, s] = jnp.dot(
+                hidden[...], down, preferred_element_type=jnp.float32
+            ).astype(part.dtype)
+
+    def finish_seq(zs):
+        total = part[0, zs, seq].astype(jnp.float32)
+        for d in range(1, n_seq):
+            peer = other_seq(d)
+            from_slice(zs, peer).wait_recv()
+            total = total + slices[zs, peer].astype(jnp.float32)
+        summed[zs] = total.astype(summed.dtype)
+
+    def step(k, carry):
+        zs = other_z(k)
+
+        @pl.when(k > 0)
+        def _():
+            for d in range(1, n_seq):
+                from_row(zs, other_seq(d)).wait_recv()
+            to_core(zs).start()
+
+        def half(j, inner):
+            @pl.when(j == 1)
+            def _():
+                from_core(zs).wait_recv()
+
+            compute(zs * 2 + lax.rem(core + j, 2), j, zs)
+            return inner
+
+        lax.fori_loop(0, 2, half, 0)
+        to_pair(zs).start()
+
+        @pl.when(k == 0)
+        def _():
+            for d in range(1, n_z):
+                source = other_z(d)
+                from_z(source).wait_recv()
+                for p in range(1, n_seq):
+                    to_row(source, p).start()
+
+        to_pair(zs).wait_recv()
+        for s in range(n_seq):
+            both = part[0, zs, s].astype(jnp.float32) + pair[zs, s].astype(jnp.float32)
+            part[0, zs, s] = both.astype(part.dtype)
+        for d in range(1, n_seq):
+            to_slice(zs, d).start()
+
+        @pl.when(k > 1)
+        def _():
+            earlier = other_z(k - 1)
+            finish_seq(earlier)
+            to_sum(earlier).start()
+
+        return carry
+
+    lax.fori_loop(0, n_z, step, 0)
+    if n_z > 1:
+        last = other_z(n_z - 1)
+        finish_seq(last)
+        to_sum(last).start()
+    finish_seq(z)
+    total = summed[z].astype(jnp.float32)
+    for d in range(1, n_z):
+        source = other_z(d)
+        from_sum(source).wait_recv()
+        total = total + columns[source].astype(jnp.float32)
+    out_ref[...] = total.astype(out_ref.dtype)
+
+    for d in range(1, n_seq):
+        from_kv(other_seq(d)).wait_recv()
+        from_label(other_seq(d)).wait_recv()
+        to_kv(d).wait_send()
+        to_label(d).wait_send()
+    for d in range(1, n_z):
+        to_z(d).wait_send()
+        to_sum(other_z(d)).wait_send()
+    for d in range(n_z):
+        zs = other_z(d)
+        to_core(zs).wait_send()
+        to_pair(zs).wait_send()
+        for p in range(1, n_seq):
+            to_slice(zs, p).wait_send()
+            if d > 0:
+                to_row(zs, p).wait_send()
+
+
+def fused_bytes(packed, w_gate, n_z, n_seq):
+    tokens, full = packed.shape
+    experts, width, ff = w_gate.shape
+    values = (2 * n_z + 1) * tokens * full + 3 * experts * width * ff + tokens * experts * ff
+    return 2 * (values + 4 * n_z * tokens * width + (2 * n_z + 1) * tokens * width // n_seq)
+
+
+def fused(packed, w_gate, w_up, w_down, kv_out, labels, n_z, n_seq):
+    tokens, full = packed.shape
+    experts, width, ff = w_gate.shape
+    out_width = width // n_seq
+    hid = experts * ff
+    bf16 = jnp.bfloat16
+    dma = pltpu.SemaphoreType.DMA
+    hbm = pl.BlockSpec(memory_space=pl.ANY)
+    vmem = pl.BlockSpec(memory_space=pltpu.VMEM)
+    return pl.pallas_call(
+        fused_kernel,
+        out_shape=(
+            jax.ShapeDtypeStruct((tokens, out_width), bf16),
+            jax.ShapeDtypeStruct(kv_out.shape, kv_out.dtype),
+            jax.ShapeDtypeStruct(labels.shape, labels.dtype),
+        ),
+        in_specs=[vmem, hbm, hbm, hbm, hbm, hbm],
+        out_specs=(vmem, hbm, hbm),
+        scratch_shapes=[
+            pltpu.VMEM((2 * n_z, tokens, full), bf16),
+            pltpu.VMEM((width, hid), bf16),
+            pltpu.VMEM((width, hid), bf16),
+            pltpu.VMEM((hid, width), bf16),
+            pltpu.VMEM((tokens, hid), bf16),
+            pltpu.VMEM((2, n_z, n_seq, tokens, out_width), bf16),
+            pltpu.VMEM((n_z, n_seq, tokens, out_width), bf16),
+            pltpu.VMEM((n_z, n_seq, tokens, out_width), bf16),
+            pltpu.VMEM((n_z, tokens, out_width), bf16),
+            pltpu.VMEM((n_z, tokens, out_width), bf16),
+            dma((3 * experts + 2,)),
+            dma((n_z,)),
+            dma((n_z,)),
+            dma((n_z, n_seq)),
+            dma((n_z, n_seq)),
+            dma((n_z,)),
+            dma((n_z,)),
+            dma((n_z,)),
+            dma((n_z,)),
+            dma((n_z, n_seq)),
+            dma((n_z, n_seq)),
+            dma((n_z,)),
+            dma((n_z,)),
+            dma((n_seq,)),
+            dma((n_seq,)),
+            dma((n_seq,)),
+            dma((n_seq,)),
+        ],
+        compiler_params=pltpu.CompilerParams(
+            collective_id=0, has_side_effects=True, vmem_limit_bytes=60 * 2**20
+        ),
+    )(packed, w_gate, w_up, w_down, kv_out, labels)
+
+
 def per_device(
     tokens,
     norm_gain,
@@ -157,6 +506,21 @@
     experts = w_gate.shape[0] * lax.axis_size("exp")
     normed = rms_normed(tokens, norm_gain)
     packed = jnp.concatenate([normed, coefficients(routes, route_weights, experts)], axis=1)
+    n_exp, n_seq = lax.axis_size("exp"), lax.axis_size("seq")
+    lanes_fit = normed.shape[1] // n_seq % LANES == 0 and w_gate.shape[2] % LANES == 0
+    rows_fit = packed.shape[0] // n_seq % 16 == 0 and n_exp % 2 == 0
+    if lanes_fit and rows_fit and fused_bytes(packed, w_gate, n_exp // 2, n_seq) < 54 * 2**20:
+        kv_out, targets = outgoing_blocks(kv_prefill, block_map, block_empty)
+        blocks = targets.shape[0]
+        per_peer = blocks // n_seq
+        labels = jnp.zeros((n_seq, -(-per_peer // 8) * 8, LANES), jnp.int32)
+        labels = labels + jnp.pad(
+            targets.reshape(n_seq, per_peer, 1), ((0, 0), (0, labels.shape[1] - per_peer), (0, 0))
+        )
+        mixed, arrived, tags = fused(
+            packed, w_gate, w_up, w_down, kv_out, labels, n_exp // 2, n_seq
+        )
+        return (mixed, put_blocks(arrived, tags[:, :per_peer, 0].reshape(blocks)))
     half = packed.shape[0] // 2
     mixed = jnp.concatenate(
         [plain(packed[i : i + half], w_gate, w_up, w_down) for i in (0, half)], axis=0

time: 377 us -> 175 us (0.46)
  waiting for transfers between devices: 239 us -> 0 us
  Pallas kernels: 12.7 us -> 163 us
  matrix products: 65.7 us -> 0 us
  local copies, waits for them, and re-layouts: 28.4 us -> 2.96 us
  between operations: 14.3 us -> 0.67 us
  starting transfers between devices: 7.35 us -> 0 us
    pallas_call x0 -> x1, Pallas kernels: none -> 150 us  [fused(): pl.pallas_call(fused_kernel, out_shape=(jax.ShapeDtypeStruct((tokens, out...]
    all_gather x2 -> x0, waiting for transfers between devices: 118 us -> none  [plain(): everyone = lax.all_gather(packed, 'exp', axis=0, tiled=True)]
    unnamed x8 -> x0, waiting for transfers between devices: 80.5 us -> none
    dot_general x8 -> x0, matrix products: 65.7 us -> none  [the longest x4 46.7 us: dense_experts(): jnp.dot(hidden.astype(jnp.bfloat16), w_down[e], preferred_element_type=jn...]
    ppermute x6 -> x0, waiting for transfers between devices: 21.6 us -> none  [passed_along(): return lax.ppermute(block, axis, route)]
    unnamed x20 -> x5, local copies, waits for them, and re-layouts: 20.8 us -> 0.73 us
    reduce_scatter x2 -> x0, waiting for transfers between devices: 18.9 us -> none  [plain(): return lax.psum_scatter(held, 'exp', scatter_dimension=0, tiled=True)]
    ppermute x6 -> x0, starting transfers between devices: 6.93 us -> none  [passed_along(): return lax.ppermute(block, axis, route)]
  transfers between devices with their start and end apart: 12 -> 0, of which waited for: 7 -> 0; matrix products, arithmetic and copies ran while one was open for 14% -> 0% of each run, Pallas kernels for 3% -> 0%
where the time goes in v2:
time: 175 us; the launch traced here: 174 us
  Pallas kernels  163 us (93%)
  other arithmetic  7.52 us (4%)
  local copies, waits for them, and re-layouts  2.96 us (2%)
    pallas_call x1, Pallas kernels, fused(): pl.pallas_call(fused_kernel, out_shape=(jax.ShapeDtypeStruct((tokens, out...  150 us
    pallas_call x1, Pallas kernels, put_blocks(): pl.pallas_call(put_kernel, out_shape=jax.ShapeDtypeStruct((layers, blocks...  6.45 us
    pallas_call x1, Pallas kernels, pick_blocks(): pl.pallas_call(pick_kernel, out_shape=jax.ShapeDtypeStruct((blocks, layer...  6.39 us

profile of v2, /device:TPU:0, one launch (start us, length us, event | category | flops | bytes accessed | tf_op | source)
XLA Modules:
  0.0 174.2 jit_solution(12790541355338563337)
XLA Ops:
  0.6 0.0 copy-start
  0.6 1.8 %fusion = f32[256]{0:T(256)S(1)} fusion(bf16[256,2560]{1,0:T(8,128)(2,1)} %param.10), kind=kLoop, calls=%fused_computation.2 | loop fusion | flops 1965824 | bytes 1311744 | tf_op jit(solution)/shard_map/reduce_sum | solution.py:19
  2.4 0.7 iota_add_fusion
  3.1 0.2 convert_reduce_fusion
  3.3 0.7 select_reduce_fusion.1
  4.0 0.1 reshape.22
  4.1 0.7 convert_element_type.17
  4.8 0.7 add.36.label_ref
  5.4 1.3 select_reduce_fusion
  6.7 0.0 copy-done
  6.7 1.1 fusion.2
  7.8 1.2 pad_maximum_fusion.packed_ref
  9.0 6.4 %shard_map.113.kv_ref = bf16[8,4,32,1024]{3,2,1,0:T(8,128)(2,1)} custom-call(s32[8]{0:T(128)} %get-tuple-element.9.order_ref, s32[8]{0:T(128)} %empty_ref.1, bf16[4,8,32,1024]{3,2,1,0:T(8,128)(2,1)} %block_ref.1), custom_call_target="tpu_custom_call" | custom-call | tf_op jit(solution)/shard_map/pallas_call | solution.py:52
  15.3 150.2 %shard_map.114 = (bf16[256,640]{1,0:T(8,128)(2,1)}, bf16[8,4,32,1024]{3,2,1,0:T(8,128)(2,1)}, s32[4,8,128]{2,1,0:T(8,128)}) custom-call(bf16[256,2688]{1,0:T(8,128)(2,1)} %pad_maximum_fusion.packed_ref, bf16[2,2560,384]{2,1,0:T(8,128)(2,1)} %w_gate_ref.1, bf16[2,2560,384]{2,1,0:T(8,128)(2,1)} %w_up_ref.1, bf16[2,384,2560]{2,1,0:T(8,128)(2,1)} %w_down_ref.1, ...), custom_call_target="tpu_custom_call" | custom-call | tf_op jit(solution)/shard_map/pallas_call | solution.py:450
  165.6 0.9 slice_reduce_fusion
  166.4 0.6 reshape_squeeze.3.slot_ref
  167.0 0.0 copy-start.1
  167.0 6.5 %shard_map.115 = bf16[4,8,32,1024]{3,2,1,0:T(8,128)(2,1)} custom-call(s32[8]{0:T(128)} %reshape_squeeze.3.slot_ref, bf16[8,4,32,1024]{3,2,1,0:T(8,128)(2,1)} %get-tuple-element.7.block_ref), custom_call_target="tpu_custom_call" | custom-call | tf_op jit(solution)/shard_map/pallas_call | solution.py:74
  173.5 0.0 copy-done.1
  173.5 0.7 copy.17
  (2 shorter events, 0.0 us)
Async XLA Ops:
  0.6 6.1 %copy-start = (bf16[256,2560]{1,0:T(8,128)(2,1)S(1)}, bf16[256,2560]{1,0:T(8,128)(2,1)}, u32[]{:S(2)}) copy-start(bf16[256,2560]{1,0:T(8,128)(2,1)} %param.10) | copy-start | bytes 3932164
  167.0 6.5 %copy-start.1 = (bf16[256,640]{1,0:T(8,128)(2,1)S(1)}, bf16[256,640]{1,0:T(8,128)(2,1)}, u32[]{:S(2)}) copy-start(bf16[256,640]{1,0:T(8,128)(2,1)} %get-tuple-element.14) | copy-start | bytes 983044
